TPU v7x, 256 devices: a whole 4x4x8 slice. The times are simulated.
256 devices in a mesh: blk: 8 (over y_lo, x), rows: 32 (over y_hi, z, core).
Axes of the slice: x: 4, y: 4 (y_hi: 2, y_lo: 2; y = y_hi * 2 + y_lo), z: 8, core: 2. Of those that a mesh axis runs over, the one named last changes fastest.
Arguments:
- embeddings: bfloat16 [524288, 768], P(('blk', 'rows')), may hold values from -6 to 6
- coverage: float32 [524288], P(('blk', 'rows')), may hold values from 0 to 4
- chosen_index: int32 [512], replicated, may hold values from 0 to 524287, as said below
- candidate_index: int32 [1024], P('blk'), may hold values from 0 to 524287, as said below
Outputs:
- new_coverage: float32 [524288], P(('blk', 'rows'))
- gains: float32 [1024], P(('blk', 'rows'))
Inputs may be any that keep to these rules, and one draw needn't show every extreme that they name: `chosen_index`: the entries are distinct; the rows r * 2048 to (r + 1) * 2048 - 1 hold at most 4 of them for every r, and exactly 4 for some r. `candidate_index`: entries b * 128 to (b + 1) * 128 - 1 lie in rows b * 65536 to (b + 1) * 65536 - 1.
All inputs are finite; a program needn't handle non-finite values.
Results may differ from a plain program's by a relative error of at most 0.00035.
Values may be sent and summed in bfloat16 or wider, within the bound.
No kernel may reach another device: no remote copies, remote signals or barrier semaphores. Data moves between devices by JAX's collectives and lax.ppermute only.
A program may use at most 64 MiB of HBM per device.

v0:
```python
import jax
import jax.numpy as jnp
from jax import lax
from jax.sharding import Mesh
from jax.sharding import PartitionSpec as P

BLK = ("blk_0", "blk_1")
BLK_ROWS = ("blk_0", "blk_1", "rows")


def in_order(pieces, dim):
    pieces = jnp.moveaxis(pieces, 0, dim)
    dims = pieces.shape
    return pieces.reshape(*dims[:dim], dims[dim] * dims[dim + 1], *dims[dim + 2 :])


def all_blocks(x, axes, sequence):
    pieces = x[None]
    for k in sequence:
        pieces = lax.all_gather(pieces, axes[k], axis=0, tiled=True)
    held = [lax.axis_size(axes[k]) for k in reversed(sequence)]
    pieces = pieces.reshape(*held, *x.shape)
    turned = sorted(range(len(sequence)), key=lambda place: sequence[len(sequence) - 1 - place])
    return pieces.transpose(*turned, *range(len(sequence), pieces.ndim)).reshape(-1, *x.shape)


def whole_of(x, axes, sequence, dim):
    return in_order(all_blocks(x, axes, sequence), dim)


def owned_rows(embeddings, indices, base_row):
    local_rows = embeddings.shape[0]
    offset = indices - base_row
    inside = (offset >= 0) & (offset < local_rows)
    safe = jnp.clip(offset, 0, local_rows - 1)
    picked = jnp.take(embeddings, safe, axis=0).astype(jnp.float32)
    return jnp.where(inside[:, None], picked, 0.0)


def local(embeddings, coverage, chosen_index, candidate_index):
    local_rows = embeddings.shape[0]
    width = embeddings.shape[1]
    scale = 1.0 / width**0.5
    device_pos = lax.axis_index(BLK) * lax.axis_size("rows") + lax.axis_index("rows")
    base_row = device_pos * local_rows
    chosen_f = lax.psum(owned_rows(embeddings, chosen_index, base_row), BLK_ROWS)
    chosen_rows = chosen_f.astype(jnp.bfloat16)
    sims = jnp.dot(embeddings, chosen_rows.T, preferred_element_type=jnp.float32) * scale
    best = jnp.max(sims, axis=1)
    new_coverage = jnp.maximum(coverage, best)
    every_index = whole_of(candidate_index, BLK, (0, 1), 0)
    every_f = lax.psum(owned_rows(embeddings, every_index, base_row), BLK_ROWS)
    every_rows = every_f.astype(jnp.bfloat16)
    cand_sims = jnp.dot(embeddings, every_rows.T, preferred_element_type=jnp.float32) * scale
    gain_part = jnp.sum(jnp.maximum(cand_sims - new_coverage[:, None], 0.0), axis=0)
    gains = lax.psum_scatter(gain_part, BLK_ROWS, scatter_dimension=0, tiled=True)
    return (new_coverage, gains)


def solution(mesh):
    torus = Mesh(mesh.devices.reshape(2, 4, mesh.shape["rows"]), ("blk_0", "blk_1", "rows"))
    return jax.shard_map(
        local,
        mesh=torus,
        in_specs=(P(BLK_ROWS, None), P(BLK_ROWS), P(), P(BLK)),
        out_specs=(P(BLK_ROWS), P(BLK_ROWS)),
        check_vma=False,
    )
```

profile of v0, /device:TPU:1, one launch (start us, length us, event | category | flops | bytes accessed | tf_op | source)
XLA Modules:
  0.0 248.3 jit_solution(17189368050249611175)
XLA Ops:
  0.6 0.0 copy-start
  0.7 0.8 compare_and_fusion.1
  1.5 1.0 copy-done
  2.5 0.0 copy-start.4
  2.5 2.7 %gather_fusion = bf16[512,768]{1,0:T(8,128)(2,1)} fusion(bf16[2048,768]{1,0:T(8,128)(2,1)S(1)} %copy-done, s32[1024]{0:T(1024)S(1)} %pad_clamp_fusion), kind=kCustom, calls=%fused_computation | custom fusion | bytes 1574912 | tf_op jit(solution)/shard_map/jit(_take)/gather | solution.py:36
  5.2 2.5 %convert_select_fusion.1 = f32[512,768]{1,0:T(8,128)} fusion(bf16[512,768]{1,0:T(8,128)(2,1)} %gather_fusion, pred[512]{0:T(512)(128)(4,1)S(1)} %get-tuple-element.4, pred[512]{0:T(512)(128)(4,1)S(1)} %get-tuple-element.6), kind=kLoop, calls=%fused_computation.6 | loop fusion | flops 1179648 | bytes 2360320 | tf_op jit(solution)/shard_map/jit(_where)/select_n | solution.py:37
  7.8 0.0 copy-done.4
  7.8 3.7 %all-gather.1 = s32[2,1,128]{2,1,0:T(1,128)S(1)} all-gather(s32[1,1,128]{2,1,0:T(1,128)S(1)} %bitcast.19), channel_id=2, replica_groups=mesh['blk_0'=2,'blk_1'=4,'rows'=32] {'blk_0'}, dimensions={0}, use_global_device_ids=true | all-gather | bytes 1536 | tf_op jit(solution)/shard_map/all_gather | solution.py:20
  11.5 7.9 %all-gather.2 = s32[4,2,128]{2,1,0:T(2,128)S(1)} all-gather(s32[1,2,128]{2,1,0:T(2,128)S(1)} %bitcast.18), channel_id=1, replica_groups=mesh['blk_0'=2,'blk_1'=4,'rows'=32] {'blk_1'}, dimensions={0}, use_global_device_ids=true | all-gather | bytes 5120 | tf_op jit(solution)/shard_map/all_gather | solution.py:20
  19.4 5.2 %gather_fusion.1 = bf16[1024,768]{1,0:T(8,128)(2,1)} fusion(bf16[2048,768]{1,0:T(8,128)(2,1)S(1)} %copy-done, s32[1024]{0:T(1024)S(1)} %broadcast_clamp_fusion), kind=kCustom, calls=%fused_computation.1 | custom fusion | bytes 3149824 | tf_op jit(solution)/shard_map/jit(_take)/gather | solution.py:36
  24.7 3.2 %convert_select_fusion = f32[1024,768]{1,0:T(8,128)} fusion(bf16[1024,768]{1,0:T(8,128)(2,1)} %gather_fusion.1, pred[1024]{0:T(1024)(128)(4,1)S(1)} %compare_and_fusion, pred[1024]{0:T(1024)(128)(4,1)S(1)} %bitcast.17), kind=kLoop, calls=%fused_computation.4 | loop fusion | flops 2359296 | bytes 4720640 | tf_op jit(solution)/shard_map/jit(_where)/select_n | solution.py:37
  27.9 138.1 %all-reduce.3 = (bf16[512,768]{1,0:T(8,128)(2,1)}, bf16[1024,768]{1,0:T(8,128)(2,1)}) all-reduce(f32[512,768]{1,0:T(8,128)} %convert_select_fusion.1, f32[1024,768]{1,0:T(8,128)} %convert_select_fusion), channel_id=1, replica_groups=mesh['blk_0'=2,'blk_1'=4,'rows'=32] {'blk_0','blk_1','rows'}, use_global_device_ids=true, to_apply=%region_0.1 | all-reduce | flops 1179648 | bytes 7077888 | tf_op jit(solution)/shard_map/psum | solution.py:46
  166.0 0.0 copy-start.1
  166.0 0.0 copy-start.3
  166.0 3.1 %multiply_reduce_fusion = f32[2048]{0:T(1024)S(1)} fusion(bf16[2048,768]{1,0:T(8,128)(2,1)S(1)} %copy-done, bf16[512,768]{1,0:T(8,128)(2,1)} %get-tuple-element.2), kind=kOutput, calls=%fused_computation.3 | convolution fusion | flops 1612707840 | bytes 3940352 | tf_op jit(solution)/shard_map/dot_general | solution.py:48
  169.1 0.0 copy-done.1
  169.1 0.0 copy-start.2
  169.2 0.0 copy-done.3
  169.2 3.9 %maximum_reduce_fusion = f32[1024]{0:T(1024)S(1)} fusion(bf16[2048,768]{1,0:T(8,128)(2,1)S(1)} %copy-done, f32[2048]{0:T(1024)S(1)} %max.18, bf16[1024,768]{1,0:T(8,128)(2,1)S(1)} %copy-done.3), kind=kOutput, calls=%fused_computation.2 | convolution fusion | flops 3229613056 | bytes 4730880 | tf_op jit(solution)/shard_map/dot_general | solution.py:54
  173.0 0.0 copy-done.2
  173.0 74.7 %all-reduce = f32[1024]{0:T(1024)S(1)} all-reduce(f32[1024]{0:T(1024)S(1)} %maximum_reduce_fusion), channel_id=3, replica_groups=mesh['blk_0'=2,'blk_1'=4,'rows'=32] {'blk_0','blk_1','rows'}, use_global_device_ids=true, to_apply=%region_4.5.clone | all-reduce | flops 1024 | bytes 8192
  247.8 0.6 dynamic-slice
  (9 shorter events, 0.1 us)
Async XLA Ops:
  0.6 1.9 copy-start
  2.5 5.3 %copy-start.4 = (s32[128]{0:T(128)S(1)}, s32[128]{0:T(128)}, u32[]{:S(2)}) copy-start(s32[128]{0:T(128)} %param.7) | copy-start | bytes 1540
  166.0 3.1 %copy-start.1 = (f32[2048]{0:T(1024)S(1)}, f32[2048]{0:T(1024)}, u32[]{:S(2)}) copy-start(f32[2048]{0:T(1024)} %param.5) | copy-start | bytes 24580
  166.0 3.1 %copy-start.3 = (bf16[1024,768]{1,0:T(8,128)(2,1)S(1)}, bf16[1024,768]{1,0:T(8,128)(2,1)}, u32[]{:S(2)}) copy-start(bf16[1024,768]{1,0:T(8,128)(2,1)} %get-tuple-element.3) | copy-start | bytes 4718596
  169.1 3.9 %copy-start.2 = (f32[2048]{0:T(1024)}, f32[2048]{0:T(1024)S(1)}, u32[]{:S(2)}) copy-start(f32[2048]{0:T(1024)S(1)} %max.18) | copy-start | bytes 24580
where the time goes:
time: 249 us; the launch traced here: 248 us
  blocking collectives  224 us (90%)
  local copies, waits for them, and re-layouts  9.6 us (4%)
  matrix products  6.95 us (3%)
  other arithmetic  6.67 us (3%)
    psum x1, blocking collectives, local(): lax.psum(owned_rows(embeddings, chosen_index, base_row), BLK_ROWS)  138 us
    unnamed x1, blocking collectives  74.7 us
    all_gather x2, blocking collectives, all_blocks(): pieces = lax.all_gather(pieces, axes[k], axis=0, tiled=True)  11.6 us
    gather x2, local copies, waits for them, and re-layouts, owned_rows(): picked = jnp.take(embeddings, safe, axis=0).astype(jnp.float32)  7.95 us
    select_n x2, other arithmetic, owned_rows(): return jnp.where(inside[:, None], picked, 0.0)  5.78 us

commit v1 on v0

--- a/solution.py
+++ b/solution.py
@@ -6,6 +6,11 @@
 
 BLK = ("blk_0", "blk_1")
 BLK_ROWS = ("blk_0", "blk_1", "rows")
+
+
+def one_after_other(value, inner_axis, outer_axis):
+    partial = lax.psum(value, inner_axis)
+    return lax.psum(partial, outer_axis)
 
 
 def in_order(pieces, dim):
@@ -43,7 +48,9 @@
     scale = 1.0 / width**0.5
     device_pos = lax.axis_index(BLK) * lax.axis_size("rows") + lax.axis_index("rows")
     base_row = device_pos * local_rows
-    chosen_f = lax.psum(owned_rows(embeddings, chosen_index, base_row), BLK_ROWS)
+    chosen_f = one_after_other(
+        owned_rows(embeddings, chosen_index, base_row), "blk_0", ("blk_1", "rows")
+    )
     chosen_rows = chosen_f.astype(jnp.bfloat16)
     sims = jnp.dot(embeddings, chosen_rows.T, preferred_element_type=jnp.float32) * scale
     best = jnp.max(sims, axis=1)

time: 249 us -> 916 us (3.68)
  blocking collectives: 224 us -> 878 us
  between operations: 0.73 us -> 14.1 us
    psum x1 -> x2, blocking collectives: 138 us -> 788 us  [the longest x1 654 us: one_after_other(): return lax.psum(partial, outer_axis)]
  transfers between devices with their start and end apart: 0 -> 1, of which waited for: 0 -> 0; matrix products, arithmetic and copies ran while one was open for 0% -> 1% of each run, Pallas kernels for 0% -> 0%
where the time goes in v1:
time: 916 us; the launch traced here: 915 us
  blocking collectives  878 us (96%)
  between operations  14.1 us (2%)
  local copies, waits for them, and re-layouts  9.54 us (1%)
    psum x1, blocking collectives, one_after_other(): return lax.psum(partial, outer_axis)  654 us
    psum x1, blocking collectives, local(): every_f = lax.psum(owned_rows(embeddings, every_index, base_row), BLK_ROWS)  134 us
    unnamed x1, blocking collectives  78.6 us
  transfers between devices with their start and end apart: 1, of which 0 were waited for; matrix products, arithmetic and copies ran while one was open for 1% of the time, Pallas kernels for 0%

profile of v1, /device:TPU:1, one launch (start us, length us, event | category | flops | bytes accessed | tf_op | source)
XLA Modules:
  0.0 915.3 jit_solution(15018406382673319933)
XLA Ops:
  7.2 0.0 copy-start
  7.2 0.0 all-reduce.5.cloned.1.call-start
  7.2 0.8 compare_and_fusion.1
  8.1 1.0 copy-done
  9.1 2.7 gather_fusion
  11.8 0.0 copy-start.4
  11.8 2.6 convert_select_fusion.1
  14.4 0.0 all-reduce.5.cloned.1.call-update
  14.4 0.0 copy-done.4
  14.4 3.7 all-gather.1
  18.1 7.9 all-gather.2
  26.1 5.2 gather_fusion.1
  31.3 3.2 convert_select_fusion
  34.5 134.1 %all-reduce.7 = bf16[1024,768]{1,0:T(8,128)(2,1)} all-reduce(f32[1024,768]{1,0:T(8,128)} %convert_select_fusion), channel_id=1, replica_groups=mesh['blk_0'=2,'blk_1'=4,'rows'=32] {'blk_0','blk_1','rows'}, use_global_device_ids=true, to_apply=%region_3.4 | all-reduce | flops 786432 | bytes 4718592 | tf_op jit(solution)/shard_map/psum | solution.py:59
  168.6 0.0 all-reduce.5.cloned.1.call-done
  168.6 653.7 %all-reduce.6 = bf16[512,768]{1,0:T(8,128)(2,1)} all-reduce(f32[512,768]{1,0:T(8,128)} %all-reduce.5.cloned.1.call-done), channel_id=1, replica_groups=mesh['blk_0'=2,'blk_1'=4,'rows'=32] {'blk_1','rows'}, use_global_device_ids=true, to_apply=%region_1.2 | all-reduce | flops 393216 | bytes 2359296 | tf_op jit(solution)/shard_map/psum | solution.py:13
  822.3 0.0 copy-start.2
  822.3 0.0 copy-start.1
  822.3 3.1 multiply_reduce_fusion
  825.4 0.0 copy-done.2
  825.4 0.0 copy-done.1
  825.4 0.0 copy-start.3
  825.4 3.9 maximum_reduce_fusion
  829.3 0.0 copy-done.3
  829.3 78.6 %all-reduce = f32[1024]{0:T(1024)S(1)} all-reduce(f32[1024]{0:T(1024)S(1)} %maximum_reduce_fusion), channel_id=3, replica_groups=mesh['blk_0'=2,'blk_1'=4,'rows'=32] {'blk_0','blk_1','rows'}, use_global_device_ids=true, to_apply=%region_5.6.clone | all-reduce | flops 1024 | bytes 8192
  907.9 0.6 dynamic-slice
  (9 shorter events, 0.1 us)
Async XLA Ops:
  7.2 1.9 copy-start
  7.2 161.5 %all-reduce.5.cloned.1.call-start = ((), (), s32[]{:S(2)}) async-start(), calls=%async_computation | async-start | bytes 3145728 | tf_op jit(solution)/shard_map/psum | solution.py:12
  11.8 2.6 copy-start.4
  822.3 3.1 copy-start.2
  822.3 3.1 copy-start.1
  825.4 3.9 copy-start.3
Sparse Core Ops, SparseCore 0:
  14.5 72.0 all-reduce.4
